TPU v7x, 32 devices: a whole 2x2x4 slice. The times are simulated.
32 devices in a mesh: req: 4 (over x, core), blk: 8 (over z, y).
Axes of the slice: x: 2, y: 2, z: 4, core: 2. Of those that a mesh axis runs over, the one named last changes fastest.
Arguments:
- queries: bfloat16 [4, 8, 512, 512], P('req', 'blk'), may hold values from -6 to 6
- keys: bfloat16 [4, 8, 512, 256], P('req', 'blk'), may hold values from -25 to 25
- values: bfloat16 [4, 8, 512, 256], P('req', 'blk'), may hold values from -6 to 6
- block_map: int32 [4, 2, 2], P('req'), may hold values from 0 to 3, as said below
- lengths: int32 [4], P('req'), may hold values from 256 to 1024
- group_of_prompt: int32 [4], replicated, may hold values from 0 to 3, each once
- decode_rank: int32 [4, 8], P('req'), may hold values from 0 to 7, as said below
Outputs:
- attended: bfloat16 [4, 8, 512, 512], P('req', 'blk')
- cache: bfloat16 [4, 1024, 2048], P('req', 'blk')
Inputs may be any that keep to these rules, and one draw needn't show every extreme that they name: In each group, block_map[g] holds each of 0 to 3 once, and the two halves of each slot hold blocks b and 3 - b, in either order. `decode_rank`: each group's row holds each of 0 to 7 once.
All inputs are finite; a program needn't handle non-finite values.
Results may differ from a plain program's by a relative error of at most 0.0098.
Values may be sent and summed in bfloat16 or wider, within the bound.
No kernel may reach another device: no remote copies, remote signals or barrier semaphores. Data moves between devices by JAX's collectives and lax.ppermute only.
A program may use at most 64 MiB of HBM per device.

v0:
```python
import math

import jax
import jax.numpy as jnp
import numpy as np
from jax import lax
from jax.experimental import pallas as pl
from jax.experimental.pallas import tpu as pltpu
from jax.sharding import PartitionSpec as P

QUERY_HEADS = 16
KEY_VALUE_HEADS = 8
HEAD_SIZE = 128
HEAD_DIVISIONS = 4
Q_DEV = 4
KV_DEV = 2
KV_WIDTH = KV_DEV * HEAD_SIZE

cap_value = 50.0
query_scale = 1.0 / 12.0
rope_base = 10000.0
VMEM_BYTES = 48 * 1024 * 1024

f32 = jnp.float32
bf16 = jnp.bfloat16
SMEM = pl.BlockSpec(memory_space=pltpu.SMEM)
VMEM = pl.BlockSpec(memory_space=pltpu.VMEM)
HBM = pl.BlockSpec(memory_space=pltpu.HBM)


def shifted(shard, axis, by):
    peers = lax.axis_size(axis)
    return lax.ppermute(shard, axis, [(i, (i + by) % peers) for i in range(peers)])


def crossed(shard, axis, by):
    peers = lax.axis_size(axis)
    return lax.ppermute(shard, axis, [(i, i ^ by) for i in range(peers)])


def rotary_tables(block_len, block_count):
    half = HEAD_SIZE // 2
    frequency = np.exp(
        np.float32(-math.log(rope_base)) * (2.0 * np.arange(half, dtype=np.float32)) / HEAD_SIZE
    ).astype(np.float64)

    def table(positions):
        angles = positions.astype(np.float64)[:, None] * frequency[None, :]
        cosine, sine = np.cos(angles), np.sin(angles)
        return np.stack(
            [np.concatenate([cosine, cosine], 1), np.concatenate([-sine, sine], 1)]
        ).astype(np.float32)

    return table(np.arange(block_len)), table(np.arange(block_count) * block_len)


def block_angles(row_table, block_table, block):
    row_cos, row_sin = row_table[0], row_table[1]
    blk_cos, blk_sin = block_table[0, pl.ds(block, 1)], block_table[1, pl.ds(block, 1)]
    return row_cos * blk_cos - row_sin * blk_sin, row_sin * blk_cos + row_cos * blk_sin


def turned(head, angles):
    x = head.astype(f32)
    return x * angles[0] + pltpu.roll(x, HEAD_SIZE // 2, 1) * angles[1]


def send_index(rank_ref, slot, head_group, row_ids, residues):
    residue = row_ids % residues
    rank = jnp.zeros_like(row_ids)
    for r in range(residues):
        rank = jnp.where(residue == r, rank_ref[0, r], rank)
    ahead = (rank - HEAD_DIVISIONS * slot + residues) % residues
    return jnp.where(ahead < HEAD_DIVISIONS, ahead ^ head_group, ahead)


def order_matrix(rank_ref, slot, head_group, out_rows, rows, residues):
    row_ids = lax.broadcasted_iota(jnp.int32, (1, rows), 1)
    ahead = send_index(rank_ref, slot, head_group, row_ids, residues)
    index = ahead * (rows // residues) + row_ids // residues
    out_ids = lax.broadcasted_iota(jnp.int32, (out_rows, rows), 0)
    return jnp.where(out_ids == index, 1.0, 0.0).astype(bf16)


def dot(a, b):
    return jnp.dot(a, b, preferred_element_type=f32)


def dot_t(a, b):
    return lax.dot_general(a, b, (((1,), (1,)), ((), ())), preferred_element_type=f32)


def expo_of(scores):
    return jnp.exp2(cap_value * math.log2(math.e) * jnp.tanh(scores * (1.0 / cap_value)))


def columns(index, width=HEAD_SIZE):
    return slice(index * width, (index + 1) * width)


def call(body, out_shape, in_specs, name, scratch=(), cost=1000):
    return pl.pallas_call(
        body,
        out_shape=out_shape,
        in_specs=in_specs,
        out_specs=jax.tree.map(lambda _: VMEM, out_shape),
        scratch_shapes=scratch,
        compiler_params=pltpu.CompilerParams(vmem_limit_bytes=VMEM_BYTES),
        cost_estimate=pl.CostEstimate(flops=cost, bytes_accessed=1000, transcendentals=0),
        name=name,
    )


def fetch(sources, targets, sems):
    copies = [pltpu.make_async_copy(s, t, sems.at[i]) for i, (s, t) in enumerate(zip(sources, targets))]
    for copy in copies:
        copy.start()
    return copies


def halves_of(map_ref, slot):
    high = jnp.where(map_ref[0, slot, 1] > map_ref[0, slot, 0], 1, 0)
    return 1 - high, high


def active_tiles(map_ref, slot, source):
    low, high = halves_of(map_ref, slot)
    source_low, source_high = halves_of(map_ref, source)
    outer = map_ref[0, slot, low] < map_ref[0, source, source_low]
    return (
        (jnp.where(outer, high, low), source_low),
        (high, jnp.where(outer, source_high, source_low)),
    )


def rows_at(index, block_len):
    return pl.ds(pl.multiple_of(index * block_len, block_len), block_len)


def own_part(queries, keys, values, table, decode_rank, owner, lens, tables):
    rows = queries.shape[0]
    block_len = rows // 2
    slots = table.shape[1]
    residues = decode_rank.shape[1]
    piece = rows // residues
    first = block_len // slots
    rest = block_len - first
    width = keys.shape[1]
    run = block_len // residues
    cache_rows = slots * piece
    groups = len(lens)
    arrays = (queries, keys, values, *tables, table, decode_rank, owner, *lens)
    count = len(arrays)

    def body(*refs):
        inputs, refs = refs[:count], refs[count:]
        qr_ref, num_ref, den_ref, select_ref, order_ref, angle_ref, place_ref, live_ref = refs[:8]
        e_refs, refs = refs[8:12], refs[12:]
        sent_refs, refs = refs[: 2 * (slots - 1)], refs[2 * (slots - 1) :]
        kr_ref, vx_ref, scratch, sems = refs[0], refs[1], refs[2 : 2 + count], refs[2 + count]
        q_ref, k_ref, v_ref, row_ref, blk_ref, map_ref, rank_ref, owner_ref = scratch[:8]
        len_refs = scratch[8:]
        copies = fetch(inputs, scratch, sems)
        member, group = lax.axis_index("blk"), lax.axis_index("req")
        slot, head_group = member // HEAD_DIVISIONS, member % HEAD_DIVISIONS

        for copy in copies[5:]:
            copy.wait()
        copies[2].wait()
        for head in range(KV_DEV):
            vx_ref[:, columns(2 * head)] = v_ref[:, columns(head)]
            vx_ref[:, columns(2 * head + 1)] = jnp.ones((rows, HEAD_SIZE), bf16)
        for turn in range(1, slots):
            order = order_matrix(
                rank_ref, (slot + turn) % slots, head_group, block_len, block_len, residues
            )
            head_ref, tail_ref = sent_refs[2 * turn - 2], sent_refs[2 * turn - 1]
            for half in range(2):
                moved = dot(order, v_ref[columns(half, block_len)]).astype(bf16)
                head_ref[columns(half, first)] = moved[:first]
                tail_ref[columns(half, rest)] = moved[first:]
        select = order_matrix(rank_ref, slot, head_group, rows // slots, rows, residues)
        select_ref[...] = select
        order_ref[...] = order_matrix(rank_ref, slot, head_group, block_len, block_len, residues)

        copies[0].wait()
        copies[1].wait()
        copies[3].wait()
        copies[4].wait()
        for half in range(2):
            part = columns(half, block_len)
            angles = block_angles(row_ref, blk_ref, map_ref[0, slot, half])
            for head in range(Q_DEV):
                qr_ref[part, columns(head)] = (
                    turned(q_ref[part, columns(head)], angles) * query_scale
                ).astype(bf16)
            for head in range(KV_DEV):
                kr_ref[part, columns(head)] = turned(k_ref[part, columns(head)], angles).astype(bf16)
            for turn in range(1, slots):
                other = block_angles(row_ref, blk_ref, map_ref[0, (slot - turn + slots) % slots, half])
                angle_ref[turn - 1, half, 0] = other[0]
                angle_ref[turn - 1, half, 1] = other[1]
        for place, source in ((0, kr_ref), (1, v_ref)):
            chosen = dot(select, source[...]).astype(bf16)
            for m in range(HEAD_DIVISIONS):
                e_refs[m][columns(place, piece)] = chosen[columns(m, piece)]

        length = 0
        for turn in range(groups):
            mine = owner_ref[lax.rem(group - turn + groups, groups)] == group
            length = length + jnp.where(mine, len_refs[turn][0], 0)
        for half in range(2):
            part = columns(half, block_len)
            start = map_ref[0, slot, half] * block_len
            live = start + lax.broadcasted_iota(jnp.int32, (block_len, 1), 0) < length
            live_ref[part] = jnp.where(live, 1.0, 0.0) + jnp.zeros((block_len, Q_DEV * HEAD_SIZE), f32)

        residue = 0
        for r in range(1, residues):
            residue = jnp.where(rank_ref[0, r] == member, r, residue)
        col = lax.broadcasted_iota(jnp.int32, (1, cache_rows), 1)
        place, offset = col // run, col % run
        target = jnp.zeros_like(col)
        for turn in range(slots):
            for half in range(2):
                block = map_ref[0, (slot - turn + slots) % slots, half]
                target = jnp.where(place == 2 * turn + half, block * run + offset, target)
        target = jnp.where(target * residues + residue < length, target, -1)
        row = lax.broadcasted_iota(jnp.int32, (cache_rows, cache_rows), 0)
        place_ref[...] = jnp.where(row == target, 1.0, 0.0).astype(bf16)

        low, high = halves_of(map_ref, slot)
        low, high = rows_at(low, block_len), rows_at(high, block_len)
        row = lax.broadcasted_iota(jnp.int32, (block_len, block_len), 0)
        col = lax.broadcasted_iota(jnp.int32, (block_len, block_len), 1)
        for head in range(Q_DEV):
            key_head = columns(head * KV_DEV // Q_DEV)

            beside = columns(head * KV_DEV // Q_DEV, 2 * HEAD_SIZE)

            def tile(q_part, k_part, diagonal):
                expo = expo_of(dot_t(qr_ref[q_part, columns(head)], kr_ref[k_part, key_head]))
                if diagonal:
                    expo = jnp.where(col <= row, expo, 0.0)
                return dot(expo.astype(bf16), vx_ref[k_part, beside])

            for q_part, sums in (
                (low, tile(low, low, True)),
                (high, tile(high, high, True) + tile(high, low, False)),
            ):
                num_ref[q_part, columns(head)] = sums[:, :HEAD_SIZE]
                den_ref[q_part, columns(head)] = sums[:, HEAD_SIZE:]

    shapes = [
        jax.ShapeDtypeStruct(queries.shape, bf16),
        jax.ShapeDtypeStruct(queries.shape, f32),
        jax.ShapeDtypeStruct(queries.shape, f32),
        jax.ShapeDtypeStruct((rows // slots, rows), bf16),
        jax.ShapeDtypeStruct((block_len, block_len), bf16),
        jax.ShapeDtypeStruct((slots - 1, 2, 2, block_len, HEAD_SIZE), f32),
        jax.ShapeDtypeStruct((cache_rows, cache_rows), bf16),
        jax.ShapeDtypeStruct(queries.shape, f32),
    ]
    shapes += [jax.ShapeDtypeStruct((2 * piece, width), bf16) for _ in range(HEAD_DIVISIONS)]
    for _ in range(1, slots):
        shapes.append(jax.ShapeDtypeStruct((2 * first, width), bf16))
        shapes.append(jax.ShapeDtypeStruct((2 * rest, width), bf16))
    scratch = [pltpu.VMEM(keys.shape, bf16), pltpu.VMEM((rows, 2 * width), bf16)]
    scratch += [pltpu.VMEM(x.shape, x.dtype) for x in arrays[:5]]
    scratch += [pltpu.SMEM(x.shape, x.dtype) for x in arrays[5:]]
    scratch.append(pltpu.SemaphoreType.DMA((count,)))
    outs = call(body, shapes, [HBM] * count, "own_part", scratch)(*arrays)
    return outs[:8], outs[8:12], outs[12:]


def other_keys(arrived, query_rot, den, select, order, angles, live, table):
    rows, width = arrived[0].shape
    block_len = rows // 2
    slots = table.shape[1]

    def body(map_ref, *refs):
        q_ref, den_ref, select_ref, order_ref, angle_ref, live_ref = refs[:6]
        refs = refs[6:]
        in_refs, refs = refs[: slots - 1], refs[slots - 1 :]
        w_refs, refs = refs[: slots - 1], refs[slots - 1 :]
        inv_ref, e_ref, k_scr, p_scr, d_scr = refs
        slot = lax.axis_index("blk") // HEAD_DIVISIONS

        d_scr[...] = den_ref[...]
        ones = jnp.ones((block_len, HEAD_SIZE), bf16)
        for turn in range(1, slots):
            source = (slot - turn + slots) % slots
            for half in range(2):
                part = columns(half, block_len)
                there = angle_ref[turn - 1, half, 0], angle_ref[turn - 1, half, 1]
                for head in range(KV_DEV):
                    k_scr[part, columns(head)] = turned(
                        in_refs[turn - 1][part, columns(head)], there
                    ).astype(bf16)
                p_scr[part] = dot(order_ref[...], k_scr[part]).astype(bf16)
            e_ref[turn - 1] = dot(select_ref[...], k_scr[...]).astype(bf16)
            for index, (half, other) in enumerate(active_tiles(map_ref, slot, source)):
                q_part, k_part = rows_at(half, block_len), rows_at(other, block_len)
                for head in range(Q_DEV):
                    key_head = columns(head * KV_DEV // Q_DEV)
                    expo = expo_of(dot_t(q_ref[q_part, columns(head)], p_scr[k_part, key_head]))
                    weight = expo.astype(bf16)
                    w_refs[turn - 1][index, head] = weight
                    d_scr[q_part, columns(head)] += dot(weight, ones)

        inv_ref[...] = live_ref[...] / d_scr[...]

    shapes = [
        jax.ShapeDtypeStruct((2, Q_DEV, block_len, block_len), bf16) for _ in range(1, slots)
    ]
    shapes.append(jax.ShapeDtypeStruct(den.shape, f32))
    shapes.append(jax.ShapeDtypeStruct((slots - 1, select.shape[0], width), bf16))
    scratch = [pltpu.VMEM((rows, width), bf16)] * 2 + [pltpu.VMEM(den.shape, f32)]
    outs = call(
        body,
        shapes,
        [SMEM] + [VMEM] * (5 + slots),
        "other_keys",
        scratch,
        cost=10**10,
    )(table, query_rot, den, select, order, angles, live, *arrived)
    return outs[: slots - 1], outs[slots - 1], outs[slots]


def late_pieces(chosen, heads):
    others, rows, width = chosen.shape
    piece = rows // HEAD_DIVISIONS
    run = piece // 2

    def body(chosen_ref, *refs):
        v_refs, e_refs = refs[:others], refs[others:]
        for m in range(HEAD_DIVISIONS):
            for index in range(others):
                e_refs[m][columns(index, piece)] = chosen_ref[index, columns(m, piece)]
                lines = [
                    v_refs[index][columns(half, 2 * piece)].astype(f32)[columns(m, run)]
                    for half in range(2)
                ]
                e_refs[m][columns(others + index, piece)] = jnp.concatenate(lines, 0).astype(bf16)

    shapes = [
        jax.ShapeDtypeStruct((2 * others * piece, width), bf16) for _ in range(HEAD_DIVISIONS)
    ]
    return call(body, shapes, [VMEM] * (1 + others), "late_pieces")(chosen, *heads)


def cache_part(early, late, place):
    cache_rows = place.shape[0]
    piece = early[0].shape[0] // 2
    width = early[0].shape[1]

    def body(place_ref, *refs):
        f_refs, s_refs, out_ref, mark_ref = refs[:4], refs[4:8], refs[8], refs[9]
        mark_ref[...] = jnp.zeros_like(mark_ref)
        head_group = lax.axis_index("blk") % HEAD_DIVISIONS
        later = cache_rows - piece
        for m in range(HEAD_DIVISIONS):
            for kind in range(2):
                lines = jnp.concatenate(
                    [f_refs[m][columns(kind, piece)], s_refs[m][columns(kind, later)]], axis=0
                )
                column = ((head_group ^ m) + kind * HEAD_DIVISIONS) * width
                out_ref[:, pl.ds(pl.multiple_of(column, HEAD_SIZE), width)] = dot(
                    place_ref[...], lines
                ).astype(bf16)

    shapes = [
        jax.ShapeDtypeStruct((cache_rows, 2 * HEAD_DIVISIONS * width), bf16),
        jax.ShapeDtypeStruct((8, HEAD_SIZE), f32),
    ]
    return call(body, shapes, [VMEM] * 9, "cache_part")(place, *early, *late)


def finish(weights, heads, tails, num, inverse, table, mark):
    rows = num.shape[0]
    block_len = rows // 2
    slots = table.shape[1]

    def body(map_ref, mark_ref, num_ref, inv_ref, *refs):
        others = slots - 1
        w_refs, h_refs, t_refs = refs[:others], refs[others : 2 * others], refs[2 * others : 3 * others]
        out_ref, v_scr, acc = refs[-3:]
        slot = lax.axis_index("blk") // HEAD_DIVISIONS
        acc[...] = num_ref[...]
        for turn in range(1, slots):
            source = (slot - turn + slots) % slots
            h_ref, t_ref, w_ref = h_refs[turn - 1], t_refs[turn - 1], w_refs[turn - 1]
            first, rest = h_ref.shape[0] // 2, t_ref.shape[0] // 2
            for other in range(2):
                v_scr[columns(other, block_len)] = jnp.concatenate(
                    [h_ref[columns(other, first)], t_ref[columns(other, rest)]], axis=0
                )
            for index, (half, other) in enumerate(active_tiles(map_ref, slot, source)):
                q_part, k_part = rows_at(half, block_len), rows_at(other, block_len)
                for head in range(Q_DEV):
                    key_head = columns(head * KV_DEV // Q_DEV)
                    acc[q_part, columns(head)] += dot(w_ref[index, head], v_scr[k_part, key_head])
        for head in range(Q_DEV):
            out_ref[:, columns(head)] = (acc[:, columns(head)] * inv_ref[:, columns(head)]).astype(bf16)

    shape = jax.ShapeDtypeStruct(num.shape, bf16)
    return call(
        body,
        shape,
        [SMEM] + [VMEM] * (3 + 3 * (slots - 1)),
        "finish",
        [pltpu.VMEM((rows, KV_WIDTH), bf16), pltpu.VMEM(num.shape, f32)],
    )(table, mark, num, inverse, *weights, *heads, *tails)


def on_device(queries, keys, values, block_map, lengths, group_of_prompt, decode_rank):
    block_len = queries.shape[2] // 2
    slots = block_map.shape[1]
    q, k, v = queries[0, 0], keys[0, 0], values[0, 0]
    tables = rotary_tables(block_len, 2 * slots)

    key_in = [shifted(k, "blk", HEAD_DIVISIONS * turn) for turn in range(1, slots)]
    lens = [lengths] + [shifted(lengths, "req", t) for t in range(1, lax.axis_size("req"))]
    (query_rot, num, den, select, order, angles, place, live), early, sent = own_part(
        q, k, v, block_map, decode_rank, group_of_prompt, lens, tables
    )
    heads = [shifted(sent[2 * t - 2], "blk", HEAD_DIVISIONS * t) for t in range(1, slots)]
    tails, key_in = lax.optimization_barrier((sent[1::2], key_in))
    tails = [shifted(tails[t - 1], "blk", HEAD_DIVISIONS * t) for t in range(1, slots)]
    early = [early[0]] + [crossed(early[m], "blk", m) for m in range(1, HEAD_DIVISIONS)]

    weights, inverse, chosen = other_keys(
        key_in, query_rot, den, select, order, angles, live, block_map
    )
    late = late_pieces(chosen, heads)
    late = [late[0]] + [crossed(late[m], "blk", m) for m in range(1, HEAD_DIVISIONS)]
    cache, mark = cache_part(early, late, place)
    attended = finish(weights, heads, tails, num, inverse, block_map, mark)
    return (attended[None, None], cache[None])


def solution(mesh):
    placed = (
        P("req", "blk", None, None),
        P("req", "blk", None, None),
        P("req", "blk", None, None),
        P("req", None, None),
        P("req"),
        P(),
        P("req", None),
    )
    return jax.shard_map(
        on_device,
        mesh=mesh,
        in_specs=placed,
        out_specs=(P("req", "blk", None, None), P("req", "blk", None)),
        check_vma=False,
    )
```

profile of v0, /device:TPU:0, one launch (start us, length us, event | category | flops | bytes accessed | tf_op | source)
XLA Modules:
  0.0 46.5 jit_solution(11338731387237953449)
XLA Ops:
  0.6 0.0 copy-start.4
  0.6 4.1 %collective-permute-start.6 = (bf16[512,256]{1,0:T(8,128)(2,1)}, bf16[512,256]{1,0:T(8,128)(2,1)S(1)}, u32[]{:S(2)}, u32[]{:S(2)}) collective-permute-start(bf16[512,256]{1,0:T(8,128)(2,1)} %bitcast.7), channel_id=1, source_target_pairs={{0,4},{1,5},{2,6},{3,7},{4,0},{5,1},{6,2},{7,3},{8,12},{9,13},{10,... | collective-permute-start | bytes 786440 | tf_op jit(solution)/shard_map/ppermute | solution.py:33
  4.7 1.5 %collective-permute-start.1 = (s32[1]{0:T(128)}, s32[1]{0:T(128)}, u32[]{:S(2)}, u32[]{:S(2)}) collective-permute-start(s32[1]{0:T(128)} %param.13), channel_id=1, source_target_pairs={{0,16},{8,24},{16,0},{24,8},{1,17},{9,25},{17,1},{25,9},{2,18},{10... | collective-permute-start | bytes 20 | tf_op jit(solution)/shard_map/ppermute | solution.py:33
  6.2 0.0 collective-permute-start
  6.2 1.7 %collective-permute-start.2 = (s32[1]{0:T(128)}, s32[1]{0:T(128)}, u32[]{:S(2)}, u32[]{:S(2)}) collective-permute-start(s32[1]{0:T(128)} %param.13), channel_id=1, source_target_pairs={{0,24},{8,0},{16,8},{24,16},{1,25},{9,1},{17,9},{25,17},{2,26},{10... | collective-permute-start | bytes 20 | tf_op jit(solution)/shard_map/ppermute | solution.py:33
  8.7 0.0 collective-permute-done.1.refs_10_
  8.7 0.6 %collective-permute-done.refs_9_ = s32[1]{0:T(128)} collective-permute-done((s32[1]{0:T(128)}, s32[1]{0:T(128)}, u32[]{:S(2)}, u32[]{:S(2)}) %collective-permute-start) | collective-permute-done | bytes 36 | tf_op jit(solution)/shard_map/ppermute | solution.py:33
  9.3 0.1 collective-permute-done.2.refs_11_
  9.4 0.0 copy-start.7
  9.4 0.0 copy-start.5
  9.4 0.0 copy-start.6
  9.4 0.0 copy-done.4
  9.4 0.6 %copy-done.7 = s32[4]{0:T(128)S(1)} copy-done((s32[4]{0:T(128)S(1)}, s32[4]{0:T(128)}, u32[]{:S(2)}) %copy-start.7) | copy-done | bytes 40
  10.1 0.0 copy-done.5
  10.1 0.0 copy-done.6
  10.1 0.0 copy-start
  10.1 1.0 %copy-done = bf16[1,1,512,512]{3,2,1,0:T(8,128)(2,1)S(1)} copy-done((bf16[1,1,512,512]{3,2,1,0:T(8,128)(2,1)S(1)}, bf16[1,1,512,512]{3,2,1,0:T(8,128)(2,1)}, u32[]{:S(2)}) %copy-start) | copy-done | bytes 524312
  11.2 0.0 copy-start.1
  11.2 0.9 %copy-done.1 = bf16[1,1,512,256]{3,2,1,0:T(8,128)(2,1)S(1)} copy-done((bf16[1,1,512,256]{3,2,1,0:T(8,128)(2,1)S(1)}, bf16[1,1,512,256]{3,2,1,0:T(8,128)(2,1)}, u32[]{:S(2)}) %copy-start.1) | copy-done | bytes 262168
  12.1 0.0 copy-start.2
  12.1 0.9 %copy-done.2 = bf16[1,1,512,256]{3,2,1,0:T(8,128)(2,1)S(1)} copy-done((bf16[1,1,512,256]{3,2,1,0:T(8,128)(2,1)S(1)}, bf16[1,1,512,256]{3,2,1,0:T(8,128)(2,1)}, u32[]{:S(2)}) %copy-start.2) | copy-done | bytes 262168
  13.1 0.0 copy-start.3
  13.1 0.9 %copy-done.3 = f32[2,256,128]{2,1,0:T(8,128)S(1)} copy-done((f32[2,256,128]{2,1,0:T(8,128)S(1)}, f32[2,256,128]{2,1,0:T(8,128)}, u32[]{:S(2)}) %copy-start.3) | copy-done | bytes 262168
  14.0 6.1 %own_part.1 = (bf16[512,512]{1,0:T(8,128)(2,1)S(1)}, f32[512,512]{1,0:T(8,128)S(1)}, f32[512,512]{1,0:T(8,128)S(1)}, bf16[256,512]{1,0:T(8,128)(2,1)S(1)}, bf16[...) custom-call(bf16[512,512]{1,0:T(8,128)(2,1)S(1)} %bitcast.5, ...), custom_call_target="tpu_custom_call" | custom-call | flops 1000 | bytes 1000 | tf_op jit(solution)/shard_map/own_part/pallas_call | solution.py:272
  20.1 1.6 %collective-permute-start.3 = (bf16[128,256]{1,0:T(8,128)(2,1)S(1)}, bf16[128,256]{1,0:T(8,128)(2,1)S(1)}, u32[]{:S(2)}, u32[]{:S(2)}) collective-permute-start(bf16[128,256]{1,0:T(8,128)(2,1)S(1)} %get-tuple-element.29), channel_id=1, source_target_pairs={{0,1},{1,0},{2,3},{3,2},{4,5},{5,4},{6,7},{7,6},{8,9},{9,8},{10,11... | collective-permute-start | bytes 196616 | tf_op jit(solution)/shard_map/ppermute | solution.py:38
  21.7 1.6 %collective-permute-start.4 = (bf16[128,256]{1,0:T(8,128)(2,1)S(1)}, bf16[128,256]{1,0:T(8,128)(2,1)S(1)}, u32[]{:S(2)}, u32[]{:S(2)}) collective-permute-start(bf16[128,256]{1,0:T(8,128)(2,1)S(1)} %get-tuple-element.30), channel_id=1, source_target_pairs={{0,2},{1,3},{2,0},{3,1},{4,6},{5,7},{6,4},{7,5},{8,10},{9,11},{10,... | collective-permute-start | bytes 196616 | tf_op jit(solution)/shard_map/ppermute | solution.py:38
  23.3 0.4 collective-permute-start.5
  23.7 0.4 collective-permute-start.7
  24.0 0.0 collective-permute-done.6.refs_6_
  24.0 2.6 %collective-permute-start.11 = (bf16[256,256]{1,0:T(8,128)(2,1)S(1)}, bf16[256,256]{1,0:T(8,128)(2,1)S(1)}, u32[]{:S(2)}, u32[]{:S(2)}) collective-permute-start(bf16[256,256]{1,0:T(8,128)(2,1)S(1)} %get-tuple-element.50), channel_id=1, source_target_pairs={{0,4},{1,5},{2,6},{3,7},{4,0},{5,1},{6,2},{7,3},{8,12},{9,13},{10,... | collective-permute-start | bytes 393224 | tf_op jit(solution)/shard_map/ppermute | solution.py:33
  26.6 0.0 copy-start.8
  26.6 1.2 %copy-done.8 = f32[512,512]{1,0:T(8,128)S(1)} copy-done((f32[512,512]{1,0:T(8,128)S(1)}, f32[512,512]{1,0:T(8,128)}, u32[]{:S(2)}) %copy-start.8) | copy-done | bytes 1048600
  27.8 2.2 %other_keys.1 = (bf16[2,4,256,256]{3,2,1,0:T(8,128)(2,1)S(1)}, f32[512,512]{1,0:T(8,128)S(1)}, bf16[1,256,256]{2,1,0:T(8,128)(2,1)S(1)}) custom-call(s32[1,2,2]{2,1,0:T(2,128)S(1)} %copy-done.5, bf16[512,512]{1,0:T(8,128)(2,1)S(1)} %get-tuple-element.32.refs_0_, f32[512,512]{1,0:T(8,128)S(1)} %get-tuple-element.33.refs_1_, ...), custom_call_target="tpu_custom_call" | custom-call | flops 10000000000 | bytes 1000 | tf_op jit(solution)/shard_map/other_keys/pallas_call | solution.py:319
  30.0 6.6 %collective-permute-done.7.refs_0_.refs_1_ = bf16[256,256]{1,0:T(8,128)(2,1)S(1)} collective-permute-done((bf16[256,256]{1,0:T(8,128)(2,1)S(1)}, bf16[256,256]{1,0:T(8,128)(2,1)S(1)}, u32[]{:S(2)}, u32[]{:S(2)}) %collective-permute-start.7) | collective-permute-done | bytes 131104 | tf_op jit(solution)/shard_map/ppermute | solution.py:33
  36.6 1.6 %collective-permute-start.8 = (bf16[128,256]{1,0:T(8,128)(2,1)S(1)}, bf16[128,256]{1,0:T(8,128)(2,1)S(1)}, u32[]{:S(2)}, u32[]{:S(2)}) collective-permute-start(bf16[128,256]{1,0:T(8,128)(2,1)S(1)} %get-tuple-element.43), channel_id=1, source_target_pairs={{0,1},{1,0},{2,3},{3,2},{4,5},{5,4},{6,7},{7,6},{8,9},{9,8},{10,11... | collective-permute-start | bytes 196616 | tf_op jit(solution)/shard_map/ppermute | solution.py:38
  38.2 0.0 collective-permute-done.3.refs_1_
  38.2 0.0 collective-permute-start.9
  38.2 0.0 collective-permute-done.4.refs_2_
  38.2 2.0 %collective-permute-start.10 = (bf16[128,256]{1,0:T(8,128)(2,1)S(1)}, bf16[128,256]{1,0:T(8,128)(2,1)S(1)}, u32[]{:S(2)}, u32[]{:S(2)}) collective-permute-start(bf16[128,256]{1,0:T(8,128)(2,1)S(1)} %get-tuple-element.45), channel_id=1, source_target_pairs={{0,3},{1,2},{2,1},{3,0},{4,7},{5,6},{6,5},{7,4},{8,11},{9,10},{10,... | collective-permute-start | bytes 196616 | tf_op jit(solution)/shard_map/ppermute | solution.py:38
  40.2 0.0 collective-permute-done.5.refs_3_
  40.2 1.2 %collective-permute-done.8.refs_5_ = bf16[128,256]{1,0:T(8,128)(2,1)S(1)} collective-permute-done((bf16[128,256]{1,0:T(8,128)(2,1)S(1)}, bf16[128,256]{1,0:T(8,128)(2,1)S(1)}, u32[]{:S(2)}, u32[]{:S(2)}) %collective-permute-start.8) | collective-permute-done | bytes 65568 | tf_op jit(solution)/shard_map/ppermute | solution.py:38
  41.4 1.1 %collective-permute-done.9.refs_6_ = bf16[128,256]{1,0:T(8,128)(2,1)S(1)} collective-permute-done((bf16[128,256]{1,0:T(8,128)(2,1)S(1)}, bf16[128,256]{1,0:T(8,128)(2,1)S(1)}, u32[]{:S(2)}, u32[]{:S(2)}) %collective-permute-start.9) | collective-permute-done | bytes 65568 | tf_op jit(solution)/shard_map/ppermute | solution.py:38
  42.5 1.0 %collective-permute-done.10.refs_7_ = bf16[128,256]{1,0:T(8,128)(2,1)S(1)} collective-permute-done((bf16[128,256]{1,0:T(8,128)(2,1)S(1)}, bf16[128,256]{1,0:T(8,128)(2,1)S(1)}, u32[]{:S(2)}, u32[]{:S(2)}) %collective-permute-start.10) | collective-permute-done | bytes 65568 | tf_op jit(solution)/shard_map/ppermute | solution.py:38
  43.4 1.1 %cache_part.1 = (bf16[128,2048]{1,0:T(8,128)(2,1)}, f32[8,128]{1,0:T(8,128)S(1)}) custom-call(bf16[128,128]{1,0:T(8,128)(2,1)S(1)} %get-tuple-element.27.place_ref, bf16[128,256]{1,0:T(8,128)(2,1)S(1)} %get-tuple-element.28.refs_0_, bf16[128,256]{1,0:T(8,128)(2,1)S(1)} %collective-permute-done.3.refs_1_, ...), custom_call_target="tpu_custom_call" | custom-call | flops 1000 | bytes 1000 | tf_op jit(solution)/shard_map/cache_part/pallas_call | solution.py:376
  44.5 0.0 collective-permute-done.11.refs_2_
  44.5 2.0 %finish.1 = bf16[512,512]{1,0:T(8,128)(2,1)} custom-call(s32[1,2,2]{2,1,0:T(2,128)S(1)} %copy-done.5, f32[8,128]{1,0:T(8,128)S(1)} %get-tuple-element.46.mark_ref, f32[512,512]{1,0:T(8,128)S(1)} %get-tuple-element.47.num_ref, f32[512,512]{1,0:T(8,128)S(1)} %get-tuple-element.48.inv_ref, bf16[2,4,256,256]{3,2,1,0:T(8,128)(2,1)S(1)} %get-tuple-element.49.refs_0_, ...), custom_call_target="tpu_custom_call" | custom-call | flops 1000 | bytes 1000 | tf_op jit(solution)/shard_map/finish/pallas_call | solution.py:407
  (1 shorter events, 0.0 us)
Async XLA Ops:
  0.6 8.8 %copy-start.4 = (f32[2,4,128]{2,1,0:T(4,128)S(1)}, f32[2,4,128]{2,1,0:T(4,128)}, u32[]{:S(2)}) copy-start(f32[2,4,128]{2,1,0:T(4,128)} %constant.5.clone.refs_4_) | copy-start | bytes 12292
  0.6 23.4 %collective-permute-start.6 = (bf16[512,256]{1,0:T(8,128)(2,1)}, bf16[512,256]{1,0:T(8,128)(2,1)S(1)}, u32[]{:S(2)}, u32[]{:S(2)}) collective-permute-start(bf16[512,256]{1,0:T(8,128)(2,1)} %bitcast.7), channel_id=1, source_target_pairs={{0,4},{1,5},{2,6},{3,7},{4,0},{5,1},{6,2},{7,3},{8,12},{9,13},{10,... | collective-permute-start | bytes 786440 | tf_op jit(solution)/shard_map/ppermute | solution.py:33
  4.7 3.9 %collective-permute-start.1 = (s32[1]{0:T(128)}, s32[1]{0:T(128)}, u32[]{:S(2)}, u32[]{:S(2)}) collective-permute-start(s32[1]{0:T(128)} %param.13), channel_id=1, source_target_pairs={{0,16},{8,24},{16,0},{24,8},{1,17},{9,25},{17,1},{25,9},{2,18},{10... | collective-permute-start | bytes 20 | tf_op jit(solution)/shard_map/ppermute | solution.py:33
  6.2 3.1 %collective-permute-start = (s32[1]{0:T(128)}, s32[1]{0:T(128)}, u32[]{:S(2)}, u32[]{:S(2)}) collective-permute-start(s32[1]{0:T(128)} %param.13), channel_id=1, source_target_pairs={{0,8},{8,16},{16,24},{24,0},{1,9},{9,17},{17,25},{25,1},{2,10},{10... | collective-permute-start | bytes 20 | tf_op jit(solution)/shard_map/ppermute | solution.py:33
  6.2 3.2 %collective-permute-start.2 = (s32[1]{0:T(128)}, s32[1]{0:T(128)}, u32[]{:S(2)}, u32[]{:S(2)}) collective-permute-start(s32[1]{0:T(128)} %param.13), channel_id=1, source_target_pairs={{0,24},{8,0},{16,8},{24,16},{1,25},{9,1},{17,9},{25,17},{2,26},{10... | collective-permute-start | bytes 20 | tf_op jit(solution)/shard_map/ppermute | solution.py:33
  9.4 0.7 %copy-start.7 = (s32[4]{0:T(128)S(1)}, s32[4]{0:T(128)}, u32[]{:S(2)}) copy-start(s32[4]{0:T(128)} %refs_7_.1) | copy-start | bytes 52
  9.4 0.7 %copy-start.5 = (s32[1,2,2]{2,1,0:T(2,128)S(1)}, s32[1,2,2]{2,1,0:T(2,128)}, u32[]{:S(2)}) copy-start(s32[1,2,2]{2,1,0:T(2,128)} %map_ref.3) | copy-start | bytes 52
  9.4 0.7 %copy-start.6 = (s32[1,8]{1,0:T(1,128)S(1)}, s32[1,8]{1,0:T(1,128)}, u32[]{:S(2)}) copy-start(s32[1,8]{1,0:T(1,128)} %refs_6_.1) | copy-start | bytes 100
  10.1 1.0 %copy-start = (bf16[1,1,512,512]{3,2,1,0:T(8,128)(2,1)S(1)}, bf16[1,1,512,512]{3,2,1,0:T(8,128)(2,1)}, u32[]{:S(2)}) copy-start(bf16[1,1,512,512]{3,2,1,0:T(8,128)(2,1)} %param.9) | copy-start | bytes 1572868
  11.2 0.9 %copy-start.1 = (bf16[1,1,512,256]{3,2,1,0:T(8,128)(2,1)S(1)}, bf16[1,1,512,256]{3,2,1,0:T(8,128)(2,1)}, u32[]{:S(2)}) copy-start(bf16[1,1,512,256]{3,2,1,0:T(8,128)(2,1)} %param.11) | copy-start | bytes 786436
  12.1 0.9 %copy-start.2 = (bf16[1,1,512,256]{3,2,1,0:T(8,128)(2,1)S(1)}, bf16[1,1,512,256]{3,2,1,0:T(8,128)(2,1)}, u32[]{:S(2)}) copy-start(bf16[1,1,512,256]{3,2,1,0:T(8,128)(2,1)} %param.10) | copy-start | bytes 786436
  13.1 0.9 %copy-start.3 = (f32[2,256,128]{2,1,0:T(8,128)S(1)}, f32[2,256,128]{2,1,0:T(8,128)}, u32[]{:S(2)}) copy-start(f32[2,256,128]{2,1,0:T(8,128)} %constant.4.clone.refs_3_) | copy-start | bytes 786436
  20.1 18.1 %collective-permute-start.3 = (bf16[128,256]{1,0:T(8,128)(2,1)S(1)}, bf16[128,256]{1,0:T(8,128)(2,1)S(1)}, u32[]{:S(2)}, u32[]{:S(2)}) collective-permute-start(bf16[128,256]{1,0:T(8,128)(2,1)S(1)} %get-tuple-element.29), channel_id=1, source_target_pairs={{0,1},{1,0},{2,3},{3,2},{4,5},{5,4},{6,7},{7,6},{8,9},{9,8},{10,11... | collective-permute-start | bytes 196616 | tf_op jit(solution)/shard_map/ppermute | solution.py:38
  21.7 16.5 %collective-permute-start.4 = (bf16[128,256]{1,0:T(8,128)(2,1)S(1)}, bf16[128,256]{1,0:T(8,128)(2,1)S(1)}, u32[]{:S(2)}, u32[]{:S(2)}) collective-permute-start(bf16[128,256]{1,0:T(8,128)(2,1)S(1)} %get-tuple-element.30), channel_id=1, source_target_pairs={{0,2},{1,3},{2,0},{3,1},{4,6},{5,7},{6,4},{7,5},{8,10},{9,11},{10,... | collective-permute-start | bytes 196616 | tf_op jit(solution)/shard_map/ppermute | solution.py:38
  23.3 16.9 %collective-permute-start.5 = (bf16[128,256]{1,0:T(8,128)(2,1)S(1)}, bf16[128,256]{1,0:T(8,128)(2,1)S(1)}, u32[]{:S(2)}, u32[]{:S(2)}) collective-permute-start(bf16[128,256]{1,0:T(8,128)(2,1)S(1)} %get-tuple-element.31), channel_id=1, source_target_pairs={{0,3},{1,2},{2,1},{3,0},{4,7},{5,6},{6,5},{7,4},{8,11},{9,10},{10,... | collective-permute-start | bytes 196616 | tf_op jit(solution)/shard_map/ppermute | solution.py:38
  23.7 12.9 %collective-permute-start.7 = (bf16[256,256]{1,0:T(8,128)(2,1)S(1)}, bf16[256,256]{1,0:T(8,128)(2,1)S(1)}, u32[]{:S(2)}, u32[]{:S(2)}) collective-permute-start(bf16[256,256]{1,0:T(8,128)(2,1)S(1)} %get-tuple-element.41), channel_id=1, source_target_pairs={{0,4},{1,5},{2,6},{3,7},{4,0},{5,1},{6,2},{7,3},{8,12},{9,13},{10,... | collective-permute-start | bytes 393224 | tf_op jit(solution)/shard_map/ppermute | solution.py:33
  24.0 20.5 %collective-permute-start.11 = (bf16[256,256]{1,0:T(8,128)(2,1)S(1)}, bf16[256,256]{1,0:T(8,128)(2,1)S(1)}, u32[]{:S(2)}, u32[]{:S(2)}) collective-permute-start(bf16[256,256]{1,0:T(8,128)(2,1)S(1)} %get-tuple-element.50), channel_id=1, source_target_pairs={{0,4},{1,5},{2,6},{3,7},{4,0},{5,1},{6,2},{7,3},{8,12},{9,13},{10,... | collective-permute-start | bytes 393224 | tf_op jit(solution)/shard_map/ppermute | solution.py:33
  26.6 1.2 %copy-start.8 = (f32[512,512]{1,0:T(8,128)S(1)}, f32[512,512]{1,0:T(8,128)}, u32[]{:S(2)}) copy-start(f32[512,512]{1,0:T(8,128)} %get-tuple-element.37.refs_5_) | copy-start | bytes 3145732
  36.6 4.8 %collective-permute-start.8 = (bf16[128,256]{1,0:T(8,128)(2,1)S(1)}, bf16[128,256]{1,0:T(8,128)(2,1)S(1)}, u32[]{:S(2)}, u32[]{:S(2)}) collective-permute-start(bf16[128,256]{1,0:T(8,128)(2,1)S(1)} %get-tuple-element.43), channel_id=1, source_target_pairs={{0,1},{1,0},{2,3},{3,2},{4,5},{5,4},{6,7},{7,6},{8,9},{9,8},{10,11... | collective-permute-start | bytes 196616 | tf_op jit(solution)/shard_map/ppermute | solution.py:38
  38.2 4.3 %collective-permute-start.9 = (bf16[128,256]{1,0:T(8,128)(2,1)S(1)}, bf16[128,256]{1,0:T(8,128)(2,1)S(1)}, u32[]{:S(2)}, u32[]{:S(2)}) collective-permute-start(bf16[128,256]{1,0:T(8,128)(2,1)S(1)} %get-tuple-element.44), channel_id=1, source_target_pairs={{0,2},{1,3},{2,0},{3,1},{4,6},{5,7},{6,4},{7,5},{8,10},{9,11},{10,... | collective-permute-start | bytes 196616 | tf_op jit(solution)/shard_map/ppermute | solution.py:38
  38.2 5.2 %collective-permute-start.10 = (bf16[128,256]{1,0:T(8,128)(2,1)S(1)}, bf16[128,256]{1,0:T(8,128)(2,1)S(1)}, u32[]{:S(2)}, u32[]{:S(2)}) collective-permute-start(bf16[128,256]{1,0:T(8,128)(2,1)S(1)} %get-tuple-element.45), channel_id=1, source_target_pairs={{0,3},{1,2},{2,1},{3,0},{4,7},{5,6},{6,5},{7,4},{8,11},{9,10},{10,... | collective-permute-start | bytes 196616 | tf_op jit(solution)/shard_map/ppermute | solution.py:38
where the time goes:
time: 46.9 us; the launch traced here: 46.5 us
  starting transfers between devices  17.4 us (37%)
  Pallas kernels  11.4 us (24%)
  waiting for transfers between devices  10.5 us (22%)
  local copies, waits for them, and re-layouts  5.81 us (12%)
  between operations  1.38 us (3%)
    ppermute x6, starting transfers between devices, shifted(): lax.ppermute(shard, axis, [(i, (i + by) % peers) for i in range(peers)])  10.3 us
    ppermute x6, waiting for transfers between devices, shifted(): lax.ppermute(shard, axis, [(i, (i + by) % peers) for i in range(peers)])  7.3 us
    ppermute x6, starting transfers between devices, crossed(): return lax.ppermute(shard, axis, [(i, i ^ by) for i in range(peers)])  7.1 us
    pallas_call x1, Pallas kernels, own_part(): outs = call(body, shapes, [HBM] * count, 'own_part', scratch)(*arrays)  6.11 us
    unnamed x18, local copies, waits for them, and re-layouts  5.81 us
    ppermute x6, waiting for transfers between devices, crossed(): return lax.ppermute(shard, axis, [(i, i ^ by) for i in range(peers)])  3.25 us
    pallas_call x1, Pallas kernels, other_keys(): call(body, shapes, [SMEM] + [VMEM] * (5 + slots), 'other_keys', scratch,...  2.2 us
    pallas_call x1, Pallas kernels, finish(): call(body, shape, [SMEM] + [VMEM] * (3 + 3 * (slots - 1)), 'finish', [plt...  2 us
  transfers between devices with their start and end apart: 12, of which 6 were waited for; matrix products, arithmetic and copies ran while one was open for 0% of the time, Pallas kernels for 20%

commit v1 on v0

--- a/solution.py
+++ b/solution.py
@@ -19,6 +19,7 @@
 cap_value = 50.0
 query_scale = 1.0 / 12.0
 rope_base = 10000.0
+CARRIED = 16
 VMEM_BYTES = 48 * 1024 * 1024
 
 f32 = jnp.float32
@@ -36,6 +37,16 @@
 def crossed(shard, axis, by):
     peers = lax.axis_size(axis)
     return lax.ppermute(shard, axis, [(i, i ^ by) for i in range(peers)])
+
+
+def spread(shard, turn):
+    groups, members = lax.axis_size("req"), lax.axis_size("blk")
+    pairs = []
+    for group in range(groups):
+        for member in range(members):
+            target = group + member % HEAD_DIVISIONS + HEAD_DIVISIONS * turn
+            pairs.append((group * members + member, target % groups * members + member))
+    return lax.ppermute(shard, ("req", "blk"), pairs)
 
 
 def rotary_tables(block_len, block_count):
@@ -109,6 +120,10 @@
         cost_estimate=pl.CostEstimate(flops=cost, bytes_accessed=1000, transcendentals=0),
         name=name,
     )
+
+
+def in_hbm(arrays):
+    return [pltpu.with_memory_space_constraint(x, pltpu.HBM) for x in arrays]
 
 
 def fetch(sources, targets, sems):
@@ -148,18 +163,21 @@
     width = keys.shape[1]
     run = block_len // residues
     cache_rows = slots * piece
-    groups = len(lens)
-    arrays = (queries, keys, values, *tables, table, decode_rank, owner, *lens)
+    groups = owner.shape[0]
+    arrays = (queries, keys, values, *tables, table, decode_rank, owner)
     count = len(arrays)
 
+    rounds = len(lens)
+
     def body(*refs):
+        len_refs, refs = refs[:rounds], refs[rounds:]
         inputs, refs = refs[:count], refs[count:]
-        qr_ref, num_ref, den_ref, select_ref, order_ref, angle_ref, place_ref, live_ref = refs[:8]
-        e_refs, refs = refs[8:12], refs[12:]
+        qr_ref, num_ref, den_ref, select_ref, order_ref, angle_ref = refs[:6]
+        place_ref, owned_ref, row_at_ref, cache_at_ref, carried_ref = refs[6:11]
+        e_refs, refs = refs[11:15], refs[15:]
         sent_refs, refs = refs[: 2 * (slots - 1)], refs[2 * (slots - 1) :]
         kr_ref, vx_ref, scratch, sems = refs[0], refs[1], refs[2 : 2 + count], refs[2 + count]
-        q_ref, k_ref, v_ref, row_ref, blk_ref, map_ref, rank_ref, owner_ref = scratch[:8]
-        len_refs = scratch[8:]
+        q_ref, k_ref, v_ref, row_ref, blk_ref, map_ref, rank_ref, owner_ref = scratch
         copies = fetch(inputs, scratch, sems)
         member, group = lax.axis_index("blk"), lax.axis_index("req")
         slot, head_group = member // HEAD_DIVISIONS, member % HEAD_DIVISIONS
@@ -205,19 +223,6 @@
             for m in range(HEAD_DIVISIONS):
                 e_refs[m][columns(place, piece)] = chosen[columns(m, piece)]
 
-        length = 0
-        for turn in range(groups):
-            mine = owner_ref[lax.rem(group - turn + groups, groups)] == group
-            length = length + jnp.where(mine, len_refs[turn][0], 0)
-        for half in range(2):
-            part = columns(half, block_len)
-            start = map_ref[0, slot, half] * block_len
-            live = start + lax.broadcasted_iota(jnp.int32, (block_len, 1), 0) < length
-            live_ref[part] = jnp.where(live, 1.0, 0.0) + jnp.zeros((block_len, Q_DEV * HEAD_SIZE), f32)
-
-        residue = 0
-        for r in range(1, residues):
-            residue = jnp.where(rank_ref[0, r] == member, r, residue)
         col = lax.broadcasted_iota(jnp.int32, (1, cache_rows), 1)
         place, offset = col // run, col % run
         target = jnp.zeros_like(col)
@@ -225,9 +230,25 @@
             for half in range(2):
                 block = map_ref[0, (slot - turn + slots) % slots, half]
                 target = jnp.where(place == 2 * turn + half, block * run + offset, target)
-        target = jnp.where(target * residues + residue < length, target, -1)
         row = lax.broadcasted_iota(jnp.int32, (cache_rows, cache_rows), 0)
         place_ref[...] = jnp.where(row == target, 1.0, 0.0).astype(bf16)
+        residue = 0
+        for r in range(1, residues):
+            residue = jnp.where(rank_ref[0, r] == member, r, residue)
+        cache_at_ref[...] = (row * residues + residue).astype(f32)
+        for half in range(2):
+            offset = lax.broadcasted_iota(jnp.int32, (block_len, HEAD_SIZE), 0)
+            row_at_ref[columns(half, block_len)] = (map_ref[0, slot, half] * block_len + offset).astype(f32)
+        line = lax.broadcasted_iota(jnp.int32, (CARRIED, width), 0)
+        carried = jnp.zeros((CARRIED, width), jnp.int32)
+        for index in range(rounds):
+            length = len_refs[index][0]
+            carried = jnp.where(line == 2 * index, lax.shift_right_logical(length, 6), carried)
+            carried = jnp.where(line == 2 * index + 1, length & 63, carried)
+        carried_ref[...] = carried.astype(f32).astype(bf16)
+        for turn in range(groups):
+            mine = owner_ref[lax.rem(group - turn + groups, groups)] == group
+            owned_ref[turn : turn + 1] = jnp.full((1, HEAD_SIZE), jnp.where(mine, 1.0, 0.0), f32)
 
         low, high = halves_of(map_ref, slot)
         low, high = rows_at(low, block_len), rows_at(high, block_len)
@@ -259,7 +280,10 @@
         jax.ShapeDtypeStruct((block_len, block_len), bf16),
         jax.ShapeDtypeStruct((slots - 1, 2, 2, block_len, HEAD_SIZE), f32),
         jax.ShapeDtypeStruct((cache_rows, cache_rows), bf16),
-        jax.ShapeDtypeStruct(queries.shape, f32),
+        jax.ShapeDtypeStruct((groups, HEAD_SIZE), f32),
+        jax.ShapeDtypeStruct((rows, HEAD_SIZE), f32),
+        jax.ShapeDtypeStruct((cache_rows, cache_rows), f32),
+        jax.ShapeDtypeStruct((CARRIED, width), bf16),
     ]
     shapes += [jax.ShapeDtypeStruct((2 * piece, width), bf16) for _ in range(HEAD_DIVISIONS)]
     for _ in range(1, slots):
@@ -269,23 +293,22 @@
     scratch += [pltpu.VMEM(x.shape, x.dtype) for x in arrays[:5]]
     scratch += [pltpu.SMEM(x.shape, x.dtype) for x in arrays[5:]]
     scratch.append(pltpu.SemaphoreType.DMA((count,)))
-    outs = call(body, shapes, [HBM] * count, "own_part", scratch)(*arrays)
-    return outs[:8], outs[8:12], outs[12:]
-
-
-def other_keys(arrived, query_rot, den, select, order, angles, live, table):
+    specs = [SMEM] * rounds + [HBM] * count
+    outs = call(body, shapes, specs, "own_part", scratch)(*lens, *in_hbm(arrays))
+    return outs[:6], outs[6:10], outs[10], outs[11:15], outs[15:]
+
+
+def other_keys(arrived, query_rot, den, select, order, angles, table):
     rows, width = arrived[0].shape
     block_len = rows // 2
     slots = table.shape[1]
 
-    def body(map_ref, *refs):
-        q_ref, den_ref, select_ref, order_ref, angle_ref, live_ref = refs[:6]
-        refs = refs[6:]
+    def body(map_hbm, q_ref, den_ref, select_ref, order_ref, angle_ref, *refs):
         in_refs, refs = refs[: slots - 1], refs[slots - 1 :]
         w_refs, refs = refs[: slots - 1], refs[slots - 1 :]
-        inv_ref, e_ref, k_scr, p_scr, d_scr = refs
+        inv_ref, e_ref, k_scr, p_scr, d_scr, map_ref, sems = refs
+        (copy,) = fetch([map_hbm], [map_ref], sems)
         slot = lax.axis_index("blk") // HEAD_DIVISIONS
-
         d_scr[...] = den_ref[...]
         ones = jnp.ones((block_len, HEAD_SIZE), bf16)
         for turn in range(1, slots):
@@ -299,41 +322,42 @@
                     ).astype(bf16)
                 p_scr[part] = dot(order_ref[...], k_scr[part]).astype(bf16)
             e_ref[turn - 1] = dot(select_ref[...], k_scr[...]).astype(bf16)
-            for index, (half, other) in enumerate(active_tiles(map_ref, slot, source)):
+            w_refs[turn - 1][...] = jnp.zeros((Q_DEV, rows, rows), bf16)
+            if turn == 1:
+                copy.wait()
+            for half, other in active_tiles(map_ref, slot, source):
                 q_part, k_part = rows_at(half, block_len), rows_at(other, block_len)
                 for head in range(Q_DEV):
                     key_head = columns(head * KV_DEV // Q_DEV)
                     expo = expo_of(dot_t(q_ref[q_part, columns(head)], p_scr[k_part, key_head]))
                     weight = expo.astype(bf16)
-                    w_refs[turn - 1][index, head] = weight
+                    w_refs[turn - 1][head, q_part, k_part] = weight
                     d_scr[q_part, columns(head)] += dot(weight, ones)
-
-        inv_ref[...] = live_ref[...] / d_scr[...]
-
-    shapes = [
-        jax.ShapeDtypeStruct((2, Q_DEV, block_len, block_len), bf16) for _ in range(1, slots)
-    ]
+        inv_ref[...] = 1.0 / d_scr[...]
+
+    shapes = [jax.ShapeDtypeStruct((Q_DEV, rows, rows), bf16) for _ in range(1, slots)]
     shapes.append(jax.ShapeDtypeStruct(den.shape, f32))
     shapes.append(jax.ShapeDtypeStruct((slots - 1, select.shape[0], width), bf16))
     scratch = [pltpu.VMEM((rows, width), bf16)] * 2 + [pltpu.VMEM(den.shape, f32)]
+    scratch += [pltpu.SMEM(table.shape, table.dtype), pltpu.SemaphoreType.DMA((1,))]
     outs = call(
         body,
         shapes,
-        [SMEM] + [VMEM] * (5 + slots),
+        [HBM] + [VMEM] * (4 + slots),
         "other_keys",
         scratch,
         cost=10**10,
-    )(table, query_rot, den, select, order, angles, live, *arrived)
+    )(*in_hbm([table]), query_rot, den, select, order, angles, *arrived)
     return outs[: slots - 1], outs[slots - 1], outs[slots]
 
 
-def late_pieces(chosen, heads):
+def late_pieces(chosen, heads, carried, early):
     others, rows, width = chosen.shape
     piece = rows // HEAD_DIVISIONS
     run = piece // 2
 
-    def body(chosen_ref, *refs):
-        v_refs, e_refs = refs[:others], refs[others:]
+    def body(carried_ref, chosen_ref, *refs):
+        v_refs, e_refs = refs[:others], refs[-HEAD_DIVISIONS:]
         for m in range(HEAD_DIVISIONS):
             for index in range(others):
                 e_refs[m][columns(index, piece)] = chosen_ref[index, columns(m, piece)]
@@ -342,75 +366,81 @@
                     for half in range(2)
                 ]
                 e_refs[m][columns(others + index, piece)] = jnp.concatenate(lines, 0).astype(bf16)
+            e_refs[m][2 * others * piece :] = carried_ref[...]
 
     shapes = [
-        jax.ShapeDtypeStruct((2 * others * piece, width), bf16) for _ in range(HEAD_DIVISIONS)
+        jax.ShapeDtypeStruct((2 * others * piece + CARRIED, width), bf16)
+        for _ in range(HEAD_DIVISIONS)
     ]
-    return call(body, shapes, [VMEM] * (1 + others), "late_pieces")(chosen, *heads)
-
-
-def cache_part(early, late, place):
+    specs = [VMEM] * (2 + others + len(early))
+    return call(body, shapes, specs, "late_pieces")(carried, chosen, *heads, *early)
+
+
+def cache_part(early, late, masks):
+    place, owned, row_at, cache_at = masks
     cache_rows = place.shape[0]
     piece = early[0].shape[0] // 2
     width = early[0].shape[1]
-
-    def body(place_ref, *refs):
-        f_refs, s_refs, out_ref, mark_ref = refs[:4], refs[4:8], refs[8], refs[9]
-        mark_ref[...] = jnp.zeros_like(mark_ref)
+    groups = owned.shape[0]
+
+    def body(place_ref, owned_ref, row_at_ref, cache_at_ref, *refs):
+        f_refs, s_refs, out_ref, live_ref = refs[:4], refs[4:8], refs[8], refs[9]
         head_group = lax.axis_index("blk") % HEAD_DIVISIONS
         later = cache_rows - piece
+        length = jnp.zeros((1, HEAD_SIZE), f32)
+        for m in range(HEAD_DIVISIONS):
+            carried = s_refs[m][2 * later :, :HEAD_SIZE].astype(f32)
+            for index in range(groups // HEAD_DIVISIONS):
+                turn = (head_group ^ m) + HEAD_DIVISIONS * index
+                value = carried[2 * index : 2 * index + 1] * 64.0 + carried[2 * index + 1 : 2 * index + 2]
+                length = length + owned_ref[pl.ds(turn, 1)] * value
+        live_ref[...] = jnp.where(row_at_ref[...] < length, 1.0, 0.0)
+        kept = jnp.where(cache_at_ref[...] < length[:, :1], place_ref[...].astype(f32), 0.0)
+        kept = kept.astype(bf16)
         for m in range(HEAD_DIVISIONS):
             for kind in range(2):
                 lines = jnp.concatenate(
                     [f_refs[m][columns(kind, piece)], s_refs[m][columns(kind, later)]], axis=0
                 )
                 column = ((head_group ^ m) + kind * HEAD_DIVISIONS) * width
-                out_ref[:, pl.ds(pl.multiple_of(column, HEAD_SIZE), width)] = dot(
-                    place_ref[...], lines
-                ).astype(bf16)
+                out_ref[:, pl.ds(pl.multiple_of(column, HEAD_SIZE), width)] = dot(kept, lines).astype(
+                    bf16
+                )
 
     shapes = [
         jax.ShapeDtypeStruct((cache_rows, 2 * HEAD_DIVISIONS * width), bf16),
-        jax.ShapeDtypeStruct((8, HEAD_SIZE), f32),
+        jax.ShapeDtypeStruct(row_at.shape, f32),
     ]
-    return call(body, shapes, [VMEM] * 9, "cache_part")(place, *early, *late)
-
-
-def finish(weights, heads, tails, num, inverse, table, mark):
+    return call(body, shapes, [VMEM] * 12, "cache_part")(*masks, *early, *late)
+
+
+def finish(weights, heads, tails, num, inverse, live):
     rows = num.shape[0]
     block_len = rows // 2
-    slots = table.shape[1]
-
-    def body(map_ref, mark_ref, num_ref, inv_ref, *refs):
-        others = slots - 1
+    others = len(weights)
+
+    def body(num_ref, inv_ref, live_ref, *refs):
         w_refs, h_refs, t_refs = refs[:others], refs[others : 2 * others], refs[2 * others : 3 * others]
-        out_ref, v_scr, acc = refs[-3:]
-        slot = lax.axis_index("blk") // HEAD_DIVISIONS
-        acc[...] = num_ref[...]
-        for turn in range(1, slots):
-            source = (slot - turn + slots) % slots
-            h_ref, t_ref, w_ref = h_refs[turn - 1], t_refs[turn - 1], w_refs[turn - 1]
-            first, rest = h_ref.shape[0] // 2, t_ref.shape[0] // 2
-            for other in range(2):
-                v_scr[columns(other, block_len)] = jnp.concatenate(
-                    [h_ref[columns(other, first)], t_ref[columns(other, rest)]], axis=0
+        out_ref, v_scr = refs[-2:]
+        for turn in range(others):
+            first, rest = h_refs[turn].shape[0] // 2, t_refs[turn].shape[0] // 2
+            for half in range(2):
+                v_scr[turn, columns(half, block_len)] = jnp.concatenate(
+                    [h_refs[turn][columns(half, first)], t_refs[turn][columns(half, rest)]], axis=0
                 )
-            for index, (half, other) in enumerate(active_tiles(map_ref, slot, source)):
-                q_part, k_part = rows_at(half, block_len), rows_at(other, block_len)
-                for head in range(Q_DEV):
-                    key_head = columns(head * KV_DEV // Q_DEV)
-                    acc[q_part, columns(head)] += dot(w_ref[index, head], v_scr[k_part, key_head])
         for head in range(Q_DEV):
-            out_ref[:, columns(head)] = (acc[:, columns(head)] * inv_ref[:, columns(head)]).astype(bf16)
+            key_head = columns(head * KV_DEV // Q_DEV)
+            total = num_ref[:, columns(head)]
+            for turn in range(others):
+                total = total + dot(w_refs[turn][head], v_scr[turn, :, key_head])
+            scale = inv_ref[:, columns(head)] * live_ref[...]
+            out_ref[:, columns(head)] = (total * scale).astype(bf16)
 
     shape = jax.ShapeDtypeStruct(num.shape, bf16)
-    return call(
-        body,
-        shape,
-        [SMEM] + [VMEM] * (3 + 3 * (slots - 1)),
-        "finish",
-        [pltpu.VMEM((rows, KV_WIDTH), bf16), pltpu.VMEM(num.shape, f32)],
-    )(table, mark, num, inverse, *weights, *heads, *tails)
+    scratch = [pltpu.VMEM((others, rows, KV_WIDTH), bf16)]
+    return call(body, shape, [VMEM] * (3 + 3 * others), "finish", scratch)(
+        num, inverse, live, *weights, *heads, *tails
+    )
 
 
 def on_device(queries, keys, values, block_map, lengths, group_of_prompt, decode_rank):
@@ -420,8 +450,8 @@
     tables = rotary_tables(block_len, 2 * slots)
 
     key_in = [shifted(k, "blk", HEAD_DIVISIONS * turn) for turn in range(1, slots)]
-    lens = [lengths] + [shifted(lengths, "req", t) for t in range(1, lax.axis_size("req"))]
-    (query_rot, num, den, select, order, angles, place, live), early, sent = own_part(
+    lens = [spread(lengths, t) for t in range(lax.axis_size("req") // HEAD_DIVISIONS)]
+    (query_rot, num, den, select, order, angles), masks, carried, early, sent = own_part(
         q, k, v, block_map, decode_rank, group_of_prompt, lens, tables
     )
     heads = [shifted(sent[2 * t - 2], "blk", HEAD_DIVISIONS * t) for t in range(1, slots)]
@@ -430,12 +460,12 @@
     early = [early[0]] + [crossed(early[m], "blk", m) for m in range(1, HEAD_DIVISIONS)]
 
     weights, inverse, chosen = other_keys(
-        key_in, query_rot, den, select, order, angles, live, block_map
-    )
-    late = late_pieces(chosen, heads)
+        key_in, query_rot, den, select, order, angles, block_map
+    )
+    late = late_pieces(chosen, heads, carried, early[1:])
     late = [late[0]] + [crossed(late[m], "blk", m) for m in range(1, HEAD_DIVISIONS)]
-    cache, mark = cache_part(early, late, place)
-    attended = finish(weights, heads, tails, num, inverse, block_map, mark)
+    cache, live = cache_part(early, late, masks)
+    attended = finish(weights, heads, tails, num, inverse, live)
     return (attended[None, None], cache[None])
 
 

time: 46.9 us -> 39.8 us (0.85)
  local copies, waits for them, and re-layouts: 5.81 us -> 0 us
  Pallas kernels: 11.4 us -> 8.85 us
  starting transfers between devices: 17.4 us -> 19.3 us
  between operations: 1.38 us -> 0.68 us
    unnamed x18 -> x0, local copies, waits for them, and re-layouts: 5.81 us -> none
    ppermute x6, starting transfers between devices: 7.1 us -> 10.5 us  [crossed(): return lax.ppermute(shard, axis, [(i, i ^ by) for i in range(peers)])]
    ppermute x6 -> x3, starting transfers between devices: 10.3 us -> 7.03 us  [shifted(): lax.ppermute(shard, axis, [(i, (i + by) % peers) for i in range(peers)])]
    pallas_call x5, Pallas kernels: 11.4 us -> 8.85 us  [the longest x1 4.32 us: own_part(): call(body, shapes, specs, 'own_part', scratch)(*lens, *in_hbm(arrays))]
    ppermute x0 -> x1, starting transfers between devices: none -> 1.81 us  [spread(): return lax.ppermute(shard, ('req', 'blk'), pairs)]
    ppermute x6 -> x3, waiting for transfers between devices: 7.3 us -> 7.23 us  [shifted(): lax.ppermute(shard, axis, [(i, (i + by) % peers) for i in range(peers)])]
  transfers between devices with their start and end apart: 12 -> 10, of which waited for: 6 -> 5; matrix products, arithmetic and copies ran while one was open for 0% -> 0% of each run, Pallas kernels for 20% -> 18%
where the time goes in v1:
time: 39.8 us; the launch traced here: 39.6 us
  starting transfers between devices  19.3 us (48%)
  waiting for transfers between devices  10.7 us (27%)
  Pallas kernels  8.85 us (22%)
  between operations  0.68 us (2%)
    ppermute x6, starting transfers between devices, crossed(): return lax.ppermute(shard, axis, [(i, i ^ by) for i in range(peers)])  10.5 us
    ppermute x3, waiting for transfers between devices, shifted(): lax.ppermute(shard, axis, [(i, (i + by) % peers) for i in range(peers)])  7.23 us
    ppermute x3, starting transfers between devices, shifted(): lax.ppermute(shard, axis, [(i, (i + by) % peers) for i in range(peers)])  7.03 us
    pallas_call x1, Pallas kernels, own_part(): call(body, shapes, specs, 'own_part', scratch)(*lens, *in_hbm(arrays))  4.32 us
    ppermute x6, waiting for transfers between devices, crossed(): return lax.ppermute(shard, axis, [(i, i ^ by) for i in range(peers)])  3.47 us
    pallas_call x1, Pallas kernels, other_keys(): call(body, shapes, [HBM] + [VMEM] * (4 + slots), 'other_keys', scratch, c...  1.83 us
    ppermute x1, starting transfers between devices, spread(): return lax.ppermute(shard, ('req', 'blk'), pairs)  1.81 us
    pallas_call x1, Pallas kernels, finish(): call(body, shape, [VMEM] * (3 + 3 * others), 'finish', scratch)  1.56 us
  transfers between devices with their start and end apart: 10, of which 5 were waited for; matrix products, arithmetic and copies ran while one was open for 0% of the time, Pallas kernels for 18%

profile of v1, /device:TPU:0, one launch (start us, length us, event | category | flops | bytes accessed | tf_op | source)
XLA Modules:
  0.0 39.6 jit_solution(17472183692560365513)
XLA Ops:
  0.6 4.1 %collective-permute-start.1 = (bf16[512,256]{1,0:T(8,128)(2,1)}, bf16[512,256]{1,0:T(8,128)(2,1)S(1)}, u32[]{:S(2)}, u32[]{:S(2)}) collective-permute-start(bf16[512,256]{1,0:T(8,128)(2,1)} %bitcast.8), channel_id=1, source_target_pairs={{0,4},{1,5},{2,6},{3,7},{4,0},{5,1},{6,2},{7,3},{8,12},{9,13},{10,... | collective-permute-start | bytes 786440 | tf_op jit(solution)/shard_map/ppermute | solution.py:34
  4.7 1.8 %collective-permute-start = (s32[1]{0:T(128)}, s32[1]{0:T(128)}, u32[]{:S(2)}, u32[]{:S(2)}) collective-permute-start(s32[1]{0:T(128)} %param.13), channel_id=1, source_target_pairs={{0,0},{1,9},{2,18},{3,27},{4,4},{5,13},{6,22},{7,31},{8,8},{9,17},... | collective-permute-start | bytes 20 | tf_op jit(solution)/shard_map/ppermute | solution.py:49
  6.5 0.0 collective-permute-done.refs_0_
  6.6 4.3 %own_part.1 = (bf16[512,512]{1,0:T(8,128)(2,1)S(1)}, f32[512,512]{1,0:T(8,128)S(1)}, f32[512,512]{1,0:T(8,128)S(1)}, bf16[256,512]{1,0:T(8,128)(2,1)S(1)}, bf16[...) custom-call(s32[1]{0:T(128)} %collective-permute-done.refs_0_, ...), custom_call_target="tpu_custom_call" | custom-call | flops 1000 | bytes 1000 | tf_op jit(solution)/shard_map/own_part/pallas_call | solution.py:297
  10.9 4.8 %collective-permute-start.2 = (bf16[128,256]{1,0:T(8,128)(2,1)S(1)}, bf16[128,256]{1,0:T(8,128)(2,1)S(1)}, u32[]{:S(2)}, u32[]{:S(2)}) collective-permute-start(bf16[128,256]{1,0:T(8,128)(2,1)S(1)} %get-tuple-element.44), channel_id=1, source_target_pairs={{0,1},{1,0},{2,3},{3,2},{4,5},{5,4},{6,7},{7,6},{8,9},{9,8},{10,11... | collective-permute-start | bytes 196616 | tf_op jit(solution)/shard_map/ppermute | solution.py:39
  15.7 0.7 %collective-permute-start.3 = (bf16[128,256]{1,0:T(8,128)(2,1)S(1)}, bf16[128,256]{1,0:T(8,128)(2,1)S(1)}, u32[]{:S(2)}, u32[]{:S(2)}) collective-permute-start(bf16[128,256]{1,0:T(8,128)(2,1)S(1)} %get-tuple-element.45), channel_id=1, source_target_pairs={{0,2},{1,3},{2,0},{3,1},{4,6},{5,7},{6,4},{7,5},{8,10},{9,11},{10,... | collective-permute-start | bytes 196616 | tf_op jit(solution)/shard_map/ppermute | solution.py:39
  16.4 1.4 %collective-permute-start.4 = (bf16[128,256]{1,0:T(8,128)(2,1)S(1)}, bf16[128,256]{1,0:T(8,128)(2,1)S(1)}, u32[]{:S(2)}, u32[]{:S(2)}) collective-permute-start(bf16[128,256]{1,0:T(8,128)(2,1)S(1)} %get-tuple-element.46), channel_id=1, source_target_pairs={{0,3},{1,2},{2,1},{3,0},{4,7},{5,6},{6,5},{7,4},{8,11},{9,10},{10,... | collective-permute-start | bytes 196616 | tf_op jit(solution)/shard_map/ppermute | solution.py:39
  17.8 0.3 collective-permute-start.5
  18.2 0.0 collective-permute-done.1.refs_0_
  18.2 2.6 %collective-permute-start.9 = (bf16[256,256]{1,0:T(8,128)(2,1)S(1)}, bf16[256,256]{1,0:T(8,128)(2,1)S(1)}, u32[]{:S(2)}, u32[]{:S(2)}) collective-permute-start(bf16[256,256]{1,0:T(8,128)(2,1)S(1)} %get-tuple-element.56), channel_id=1, source_target_pairs={{0,4},{1,5},{2,6},{3,7},{4,0},{5,1},{6,2},{7,3},{8,12},{9,13},{10,... | collective-permute-start | bytes 393224 | tf_op jit(solution)/shard_map/ppermute | solution.py:34
  20.8 1.8 %other_keys.1 = (bf16[4,512,512]{2,1,0:T(8,128)(2,1)S(1)}, f32[512,512]{1,0:T(8,128)S(1)}, bf16[1,256,256]{2,1,0:T(8,128)(2,1)S(1)}) custom-call(s32[1,2,2]{2,1,0:T(2,128)} %map_hbm.1, bf16[512,512]{1,0:T(8,128)(2,1)S(1)} %get-tuple-element.31.q_ref, f32[512,512]{1,0:T(8,128)S(1)} %get-tuple-element.32.den_ref, ...), custom_call_target="tpu_custom_call" | custom-call | flops 10000000000 | bytes 1000 | tf_op jit(solution)/shard_map/other_keys/pallas_call | solution.py:343
  22.6 0.0 collective-permute-done.2.refs_1_
  22.6 0.0 collective-permute-done.3.refs_2_
  22.6 0.3 collective-permute-done.4.refs_3_
  22.9 7.2 %collective-permute-done.5.refs_0_.refs_1_ = bf16[256,256]{1,0:T(8,128)(2,1)S(1)} collective-permute-done((bf16[256,256]{1,0:T(8,128)(2,1)S(1)}, bf16[256,256]{1,0:T(8,128)(2,1)S(1)}, u32[]{:S(2)}, u32[]{:S(2)}) %collective-permute-start.5) | collective-permute-done | bytes 131104 | tf_op jit(solution)/shard_map/ppermute | solution.py:34
  30.2 1.4 %collective-permute-start.6 = (bf16[144,256]{1,0:T(8,128)(2,1)S(1)}, bf16[144,256]{1,0:T(8,128)(2,1)S(1)}, u32[]{:S(2)}, u32[]{:S(2)}) collective-permute-start(bf16[144,256]{1,0:T(8,128)(2,1)S(1)} %get-tuple-element.51), channel_id=1, source_target_pairs={{0,1},{1,0},{2,3},{3,2},{4,5},{5,4},{6,7},{7,6},{8,9},{9,8},{10,11... | collective-permute-start | bytes 221192 | tf_op jit(solution)/shard_map/ppermute | solution.py:39
  31.6 0.0 collective-permute-start.7
  31.6 2.1 %collective-permute-start.8 = (bf16[144,256]{1,0:T(8,128)(2,1)S(1)}, bf16[144,256]{1,0:T(8,128)(2,1)S(1)}, u32[]{:S(2)}, u32[]{:S(2)}) collective-permute-start(bf16[144,256]{1,0:T(8,128)(2,1)S(1)} %get-tuple-element.53), channel_id=1, source_target_pairs={{0,3},{1,2},{2,1},{3,0},{4,7},{5,6},{6,5},{7,4},{8,11},{9,10},{10,... | collective-permute-start | bytes 221192 | tf_op jit(solution)/shard_map/ppermute | solution.py:39
  33.7 1.1 %collective-permute-done.6.refs_5_ = bf16[144,256]{1,0:T(8,128)(2,1)S(1)} collective-permute-done((bf16[144,256]{1,0:T(8,128)(2,1)S(1)}, bf16[144,256]{1,0:T(8,128)(2,1)S(1)}, u32[]{:S(2)}, u32[]{:S(2)}) %collective-permute-start.6) | collective-permute-done | bytes 73760 | tf_op jit(solution)/shard_map/ppermute | solution.py:39
  34.9 1.1 %collective-permute-done.7.refs_6_ = bf16[144,256]{1,0:T(8,128)(2,1)S(1)} collective-permute-done((bf16[144,256]{1,0:T(8,128)(2,1)S(1)}, bf16[144,256]{1,0:T(8,128)(2,1)S(1)}, u32[]{:S(2)}, u32[]{:S(2)}) %collective-permute-start.7) | collective-permute-done | bytes 73760 | tf_op jit(solution)/shard_map/ppermute | solution.py:39
  36.0 0.9 %collective-permute-done.8.refs_7_ = bf16[144,256]{1,0:T(8,128)(2,1)S(1)} collective-permute-done((bf16[144,256]{1,0:T(8,128)(2,1)S(1)}, bf16[144,256]{1,0:T(8,128)(2,1)S(1)}, u32[]{:S(2)}, u32[]{:S(2)}) %collective-permute-start.8) | collective-permute-done | bytes 73760 | tf_op jit(solution)/shard_map/ppermute | solution.py:39
  36.9 1.1 %cache_part.1 = (bf16[128,2048]{1,0:T(8,128)(2,1)}, f32[512,128]{1,0:T(8,128)S(1)}) custom-call(bf16[128,128]{1,0:T(8,128)(2,1)S(1)} %get-tuple-element.39.place_ref, f32[4,128]{1,0:T(4,128)S(1)} %get-tuple-element.40.owned_ref, f32[512,128]{1,0:T(8,128)S(1)} %get-tuple-element.41.row_at_ref, f32[128,128]{1,0:T(8,128)S(1)} %get-tuple-element.42.cache_at_ref, ...), custom_call_target="tpu_custom_call" | custom-call | flops 1000 | bytes 1000 | tf_op jit(solution)/shard_map/cache_part/pallas_call | solution.py:414
  38.0 0.0 collective-permute-done.9.refs_2_
  38.0 1.6 %finish.1 = bf16[512,512]{1,0:T(8,128)(2,1)} custom-call(f32[512,512]{1,0:T(8,128)S(1)} %get-tuple-element.30.num_ref, f32[512,512]{1,0:T(8,128)S(1)} %get-tuple-element.38.inv_ref, f32[512,128]{1,0:T(8,128)S(1)} %get-tuple-element.54.live_ref, bf16[4,512,512]{2,1,0:T(8,128)(2,1)S(1)} %get-tuple-element.55.refs_0_, ...), custom_call_target="tpu_custom_call" | custom-call | flops 1000 | bytes 1000 | tf_op jit(solution)/shard_map/finish/pallas_call | solution.py:441
  (1 shorter events, 0.0 us)
Async XLA Ops:
  0.6 17.5 %collective-permute-start.1 = (bf16[512,256]{1,0:T(8,128)(2,1)}, bf16[512,256]{1,0:T(8,128)(2,1)S(1)}, u32[]{:S(2)}, u32[]{:S(2)}) collective-permute-start(bf16[512,256]{1,0:T(8,128)(2,1)} %bitcast.8), channel_id=1, source_target_pairs={{0,4},{1,5},{2,6},{3,7},{4,0},{5,1},{6,2},{7,3},{8,12},{9,13},{10,... | collective-permute-start | bytes 786440 | tf_op jit(solution)/shard_map/ppermute | solution.py:34
  4.7 1.8 %collective-permute-start = (s32[1]{0:T(128)}, s32[1]{0:T(128)}, u32[]{:S(2)}, u32[]{:S(2)}) collective-permute-start(s32[1]{0:T(128)} %param.13), channel_id=1, source_target_pairs={{0,0},{1,9},{2,18},{3,27},{4,4},{5,13},{6,22},{7,31},{8,8},{9,17},... | collective-permute-start | bytes 20 | tf_op jit(solution)/shard_map/ppermute | solution.py:49
  10.9 11.7 %collective-permute-start.2 = (bf16[128,256]{1,0:T(8,128)(2,1)S(1)}, bf16[128,256]{1,0:T(8,128)(2,1)S(1)}, u32[]{:S(2)}, u32[]{:S(2)}) collective-permute-start(bf16[128,256]{1,0:T(8,128)(2,1)S(1)} %get-tuple-element.44), channel_id=1, source_target_pairs={{0,1},{1,0},{2,3},{3,2},{4,5},{5,4},{6,7},{7,6},{8,9},{9,8},{10,11... | collective-permute-start | bytes 196616 | tf_op jit(solution)/shard_map/ppermute | solution.py:39
  15.7 6.9 %collective-permute-start.3 = (bf16[128,256]{1,0:T(8,128)(2,1)S(1)}, bf16[128,256]{1,0:T(8,128)(2,1)S(1)}, u32[]{:S(2)}, u32[]{:S(2)}) collective-permute-start(bf16[128,256]{1,0:T(8,128)(2,1)S(1)} %get-tuple-element.45), channel_id=1, source_target_pairs={{0,2},{1,3},{2,0},{3,1},{4,6},{5,7},{6,4},{7,5},{8,10},{9,11},{10,... | collective-permute-start | bytes 196616 | tf_op jit(solution)/shard_map/ppermute | solution.py:39
  16.4 6.5 %collective-permute-start.4 = (bf16[128,256]{1,0:T(8,128)(2,1)S(1)}, bf16[128,256]{1,0:T(8,128)(2,1)S(1)}, u32[]{:S(2)}, u32[]{:S(2)}) collective-permute-start(bf16[128,256]{1,0:T(8,128)(2,1)S(1)} %get-tuple-element.46), channel_id=1, source_target_pairs={{0,3},{1,2},{2,1},{3,0},{4,7},{5,6},{6,5},{7,4},{8,11},{9,10},{10,... | collective-permute-start | bytes 196616 | tf_op jit(solution)/shard_map/ppermute | solution.py:39
  17.8 12.3 %collective-permute-start.5 = (bf16[256,256]{1,0:T(8,128)(2,1)S(1)}, bf16[256,256]{1,0:T(8,128)(2,1)S(1)}, u32[]{:S(2)}, u32[]{:S(2)}) collective-permute-start(bf16[256,256]{1,0:T(8,128)(2,1)S(1)} %get-tuple-element.49), channel_id=1, source_target_pairs={{0,4},{1,5},{2,6},{3,7},{4,0},{5,1},{6,2},{7,3},{8,12},{9,13},{10,... | collective-permute-start | bytes 393224 | tf_op jit(solution)/shard_map/ppermute | solution.py:34
  18.2 19.8 %collective-permute-start.9 = (bf16[256,256]{1,0:T(8,128)(2,1)S(1)}, bf16[256,256]{1,0:T(8,128)(2,1)S(1)}, u32[]{:S(2)}, u32[]{:S(2)}) collective-permute-start(bf16[256,256]{1,0:T(8,128)(2,1)S(1)} %get-tuple-element.56), channel_id=1, source_target_pairs={{0,4},{1,5},{2,6},{3,7},{4,0},{5,1},{6,2},{7,3},{8,12},{9,13},{10,... | collective-permute-start | bytes 393224 | tf_op jit(solution)/shard_map/ppermute | solution.py:34
  30.2 4.7 %collective-permute-start.6 = (bf16[144,256]{1,0:T(8,128)(2,1)S(1)}, bf16[144,256]{1,0:T(8,128)(2,1)S(1)}, u32[]{:S(2)}, u32[]{:S(2)}) collective-permute-start(bf16[144,256]{1,0:T(8,128)(2,1)S(1)} %get-tuple-element.51), channel_id=1, source_target_pairs={{0,1},{1,0},{2,3},{3,2},{4,5},{5,4},{6,7},{7,6},{8,9},{9,8},{10,11... | collective-permute-start | bytes 221192 | tf_op jit(solution)/shard_map/ppermute | solution.py:39
  31.6 4.4 %collective-permute-start.7 = (bf16[144,256]{1,0:T(8,128)(2,1)S(1)}, bf16[144,256]{1,0:T(8,128)(2,1)S(1)}, u32[]{:S(2)}, u32[]{:S(2)}) collective-permute-start(bf16[144,256]{1,0:T(8,128)(2,1)S(1)} %get-tuple-element.52), channel_id=1, source_target_pairs={{0,2},{1,3},{2,0},{3,1},{4,6},{5,7},{6,4},{7,5},{8,10},{9,11},{10,... | collective-permute-start | bytes 221192 | tf_op jit(solution)/shard_map/ppermute | solution.py:39
  31.6 5.3 %collective-permute-start.8 = (bf16[144,256]{1,0:T(8,128)(2,1)S(1)}, bf16[144,256]{1,0:T(8,128)(2,1)S(1)}, u32[]{:S(2)}, u32[]{:S(2)}) collective-permute-start(bf16[144,256]{1,0:T(8,128)(2,1)S(1)} %get-tuple-element.53), channel_id=1, source_target_pairs={{0,3},{1,2},{2,1},{3,0},{4,7},{5,6},{6,5},{7,4},{8,11},{9,10},{10,... | collective-permute-start | bytes 221192 | tf_op jit(solution)/shard_map/ppermute | solution.py:39
